TPU v7x, 32 devices: a whole 2x2x4 slice. The times are simulated.
32 devices in a mesh: groups: 2 (over y), tensor: 8 (over z, x), store: 2 (over core).
Axes of the slice: x: 2, y: 2, z: 4, core: 2. Of those that a mesh axis runs over, the one named last changes fastest.
Arguments:
- inputs: bfloat16 [4, 1024, 8192], P('groups', 'store', 'tensor'), parts along dimension 0, may hold values from -6 to 6
- base_up_matrix: bfloat16 [8192, 28672], P(None, 'tensor'), may hold values from -0.0625 to 0.0625
- adapter_shrink_weight: bfloat16 [64, 64, 8192], P('store', None, 'tensor'), may hold values from -0.0625 to 0.0625
- adapter_expand_weight: bfloat16 [64, 64, 28672], P('store', None, 'tensor'), may hold values from -0.75 to 0.75
- block_adapter_index: int32 [4, 8], P('groups'), parts along dimension 0, may hold values from 0 to 63
Outputs:
- projected: bfloat16 [4, 1024, 28672], P('groups', 'store', 'tensor'), parts along dimension 0
There are 2 independent parts, one for each index of `groups`. A program takes and returns all parts, laid end to end along the dimension named above; an argument that names none is the same for every part. Nothing has to cross between parts.
All inputs are finite; a program needn't handle non-finite values.
Results may differ from a plain program's by a relative error of at most 0.0038.
Values may be sent and summed in bfloat16 or wider, within the bound.
A program may use at most 256 MiB of HBM per device.

v0:
```python
import jax
import jax.numpy as jnp
from jax import lax
from jax.sharding import PartitionSpec as P


def local(
    inputs, base_up_matrix, adapter_shrink_weight, adapter_expand_weight, block_adapter_index
):
    step_count, rows_dev, width_dev = inputs.shape
    hidden_dev = base_up_matrix.shape[1]
    store_count = lax.axis_size("store")
    my_rank = lax.axis_index("store")
    adapters_held_count = adapter_shrink_weight.shape[0]
    blocks_dev = block_adapter_index.shape[1] // store_count
    block_rows = rows_dev // blocks_dev
    wanted = block_adapter_index.reshape(step_count, store_count, blocks_dev).transpose(1, 0, 2)
    owner_rank = wanted // adapters_held_count
    local_adapter_index = wanted % adapters_held_count
    owned_locally = (owner_rank == my_rank)[..., None, None]
    send_down = jnp.where(
        owned_locally,
        jnp.take(adapter_shrink_weight, local_adapter_index, axis=0),
        jnp.zeros((), jnp.bfloat16),
    )
    expand_transfer = jnp.where(
        owned_locally,
        jnp.take(adapter_expand_weight, local_adapter_index, axis=0),
        jnp.zeros((), jnp.bfloat16),
    )
    got_down, got_up = (
        lax.all_to_all(send_down, "store", split_axis=0, concat_axis=0, tiled=True),
        lax.all_to_all(expand_transfer, "store", split_axis=0, concat_axis=0, tiled=True),
    )
    shrink_matrices = jnp.sum(got_down.astype(jnp.float32), axis=0).astype(jnp.bfloat16)
    expand_matrices = jnp.sum(got_up.astype(jnp.float32), axis=0).astype(jnp.bfloat16)
    flat_rows = inputs.reshape(step_count * rows_dev, width_dev)
    full_rows, full_down = (
        lax.all_gather(flat_rows, "tensor", axis=1, tiled=True),
        lax.all_gather(shrink_matrices, "tensor", axis=3, tiled=True),
    )
    base_out = jnp.dot(full_rows, base_up_matrix, preferred_element_type=jnp.float32)
    row_blocks = full_rows.reshape(step_count, blocks_dev, block_rows, full_rows.shape[1])
    low_rank = jnp.einsum(
        "sbtd,sbrd->sbrt", row_blocks, full_down, preferred_element_type=jnp.float32
    )
    low_rank = low_rank.astype(jnp.bfloat16)
    adapter_out = jnp.einsum(
        "sbrt,sbrf->sbtf", low_rank, expand_matrices, preferred_element_type=jnp.float32
    )
    adapter_out = adapter_out.reshape(step_count * rows_dev, hidden_dev)
    projected = (base_out + adapter_out).astype(jnp.bfloat16)
    return projected.reshape(step_count, rows_dev, hidden_dev)


def solution(mesh):
    placed = (
        P("groups", "store", "tensor"),
        P(None, "tensor"),
        P("store", None, "tensor"),
        P("store", None, "tensor"),
        P("groups", None),
    )
    return jax.shard_map(
        local, mesh=mesh, in_specs=placed, out_specs=P("groups", "store", "tensor"), check_vma=False
    )
```

profile of v0, /device:TPU:0, one launch (start us, length us, event | category | flops | bytes accessed | tf_op | source)
XLA Modules:
  0.0 468.0 jit_solution(10533825671606190951)
XLA Ops:
  6.5 0.0 all-gather.5.cloned.1.call-start
  6.5 0.8 reshape.22
  7.4 0.1 reshape.28
  7.4 2.9 gather_fusion
  10.3 0.3 select_select_fusion.1
  10.6 5.4 %all_to_all.10 = bf16[2,2,4,64,1024]{4,3,2,1,0:T(8,128)(2,1)S(1)} all-to-all(bf16[2,2,4,64,1024]{4,3,2,1,0:T(8,128)(2,1)S(1)} %select_select_fusion.1), channel_id=1, replica_groups=mesh['groups'=2,'tensor'=8,'store'=2] {'store'}, dimensions={0} | all-to-all | bytes 4194304 | tf_op jit(solution)/shard_map/all_to_all | solution.py:32
  16.0 1.7 reduce_sum.24
  17.8 0.0 all-gather.5.cloned.1.call-update
  17.8 0.0 all-gather.3.cloned.1.call-start
  17.9 0.7 all-gather.3.cloned.1.call-update
  18.6 9.2 %gather_fusion.1 = bf16[16,64,3584]{2,1,0:T(8,128)(2,1)} fusion(bf16[32,64,3584]{2,1,0:T(8,128)(2,1)} %param.8, s32[1024]{0:T(1024)S(1)} %pad_clamp_fusion), kind=kCustom, calls=%fused_computation.1 | custom fusion | bytes 14680128 | tf_op jit(solution)/shard_map/jit(_take)/gather | solution.py:28
  27.8 4.7 %select_select_fusion = bf16[2,2,4,64,3584]{4,3,2,1,0:T(8,128)(2,1)S(1)} fusion(bf16[2,2,4,64,3584]{4,3,2,1,0:T(8,128)(2,1)} %bitcast.37, pred[2,2,4]{2,1,0:T(4,128)(4,1)S(1)} %copy.7, pred[2,2,4]{2,1,0:T(4,128)(4,1)S(1)} %copy.6), kind=kLoop, calls=%fused_computation.4 | loop fusion | flops 7340032 | bytes 14680096 | tf_op jit(solution)/shard_map/jit(_where)/select_n | solution.py:26
  32.5 10.9 %all_to_all.11 = bf16[2,2,4,64,3584]{4,3,2,1,0:T(8,128)(2,1)} all-to-all(bf16[2,2,4,64,3584]{4,3,2,1,0:T(8,128)(2,1)S(1)} %select_select_fusion), channel_id=1, replica_groups=mesh['groups'=2,'tensor'=8,'store'=2] {'store'}, dimensions={0} | all-to-all | bytes 14680064 | tf_op jit(solution)/shard_map/all_to_all | solution.py:33
  43.4 7.3 %reduce_sum.25 = bf16[2,4,64,3584]{3,2,1,0:T(8,128)(2,1)} reduce(bf16[2,2,4,64,3584]{4,3,2,1,0:T(8,128)(2,1)} %all_to_all.11, bf16[]{:T(256)} %constant.61.clone.1), dimensions={0}, to_apply=%region_1.2 | reduce | flops 1835008 | bytes 11010050 | tf_op jit(solution)/shard_map/reduce_sum | solution.py:36
  50.7 94.9 %all-gather.5.cloned.1.call-done = bf16[2,4,64,8192]{3,2,1,0:T(8,128)(2,1)} async-done(((bf16[2,4,64,1024]{3,2,1,0:T(8,128)(2,1)}), bf16[2,4,64,8192]{3,2,1,0:T(8,128)(2,1)}) %all-gather.5.cloned.1.call-update) | async-done | bytes 8388624 | tf_op jit(solution)/shard_map/all_gather | solution.py:40
  145.6 228.0 %all-gather.3.cloned.1.call-done = bf16[1024,8192]{1,0:T(8,128)(2,1)} async-done(((bf16[1024,1024]{1,0:T(8,128)(2,1)}), bf16[1024,8192]{1,0:T(8,128)(2,1)}) %all-gather.3.cloned.1.call-update) | async-done | bytes 16777232 | tf_op jit(solution)/shard_map/all_gather | solution.py:39
  373.6 16.2 %fusion.1 = f32[2,4,128,3584]{3,2,1,0:T(8,128)} fusion(bf16[2,4,64,3584]{3,2,1,0:T(8,128)(2,1)} %reduce_sum.25, bf16[2,4,64,8192]{3,2,1,0:T(8,128)(2,1)} %all-gather.5.cloned.1.call-done, bf16[2,4,128,8192]{3,2,1,0:T(8,128)(2,1)} %bitcast.38), kind=kOutput, calls=%fused_computation.7 | convolution fusion | flops 1543569408 | bytes 43515904 | tf_op jit(solution)/shard_map/sbrt,sbrf->sbtf/dot_general | solution.py:48
  389.8 71.5 %fusion = bf16[1024,3584]{1,0:T(8,128)(2,1)} fusion(f32[2,4,128,3584]{3,2,1,0:T(8,128)} %fusion.1, bf16[1024,8192]{1,0:T(8,128)(2,1)} %all-gather.3.cloned.1.call-done, bf16[8192,3584]{1,0:T(8,128)(2,1)} %param.6), kind=kOutput, calls=%fused_computation.3 | convolution fusion | flops 60136882176 | bytes 97517568 | tf_op jit(solution)/shard_map/dot_general | solution.py:42
  (5 shorter events, 0.0 us)
Async XLA Ops:
  6.5 139.0 %all-gather.5.cloned.1.call-start = ((), (), s32[]{:S(2)}) async-start(), calls=%async_computation.3 | async-start | bytes 9437184 | tf_op jit(solution)/shard_map/all_gather | solution.py:40
  17.8 355.8 %all-gather.3.cloned.1.call-start = ((), (), s32[]{:S(2)}) async-start(), calls=%async_computation.2 | async-start | bytes 18874368 | tf_op jit(solution)/shard_map/all_gather | solution.py:39
Sparse Core Ops, SparseCore 0:
  17.9 127.5 all-gather.4
  147.8 225.7 all-gather.2
where the time goes:
time: 468 us
  waiting for transfers between devices  324 us (69%)
  matrix products  87.6 us (19%)
  blocking collectives  16.3 us (3%)
  other arithmetic  14.1 us (3%)
  between operations  13.4 us (3%)
  local copies, waits for them, and re-layouts  13 us (3%)
    all_gather x1, waiting for transfers between devices, local(): lax.all_gather(flat_rows, 'tensor', axis=1, tiled=True)  228 us
    all_gather x1, waiting for transfers between devices, local(): lax.all_gather(shrink_matrices, 'tensor', axis=3, tiled=True)  94.9 us
    dot_general x1, matrix products, local(): jnp.dot(full_rows, base_up_matrix, preferred_element_type=jnp.float32)  71.5 us
    dot_general x1, matrix products, local(): jnp.einsum('sbrt,sbrf->sbtf', low_rank, expand_matrices, preferred_elemen...  16.2 us
    all_to_all x1, blocking collectives, local(): lax.all_to_all(expand_transfer, 'store', split_axis=0, concat_axis=0, til...  10.9 us
  transfers between devices with their start and end apart: 2, of which 2 were waited for; matrix products, arithmetic and copies ran while one was open for 5% of the time, Pallas kernels for 0%

commit v1 on v0

v1 whole, which is shorter than its diff:
```python
import functools

import jax
import jax.numpy as jnp
from jax import lax
from jax.experimental import pallas as pl
from jax.experimental.pallas import tpu as pltpu
from jax.sharding import PartitionSpec as P

MESH = pl.DeviceIdType.MESH
F32 = jnp.float32
BF16 = jnp.bfloat16
PIECES = 8
TILE = 256


def kernel(
    x_ref, base_ref, down_mine, down_send, up_mine, up_send,
    out_ref,
    xbuf, total, wbuf, down, up, part, gathered, ranks,
    send_sem, recv_sem, w_sem, local_sem, pair_send, pair_recv,
    rs_send, rs_recv, ag_send, ag_recv, out_sem,
):
    n = lax.axis_size("tensor")
    t = lax.axis_index("tensor")
    core = lax.axis_index("store")
    z, x = t // 2, t % 2
    sign = jnp.where(z < 2, 1, -1)
    is_end = (z == 0) | (z == 3)
    far, near, across = t + 2 * sign, t - 2 * sign, z * 2 + 1 - x
    rank = down.shape[1] // 2
    depth = xbuf.shape[2]
    tiles = total.shape[1] // TILE

    barrier = pltpu.get_barrier_semaphore()
    for d in range(1, n):
        pl.semaphore_signal(
            barrier, inc=1, device_id={"tensor": lax.rem(t + d, n)}, device_id_type=MESH
        )
    pl.semaphore_signal(barrier, inc=1, device_id={"store": 1 - core}, device_id_type=MESH)

    own_x = pltpu.make_async_copy(x_ref, xbuf.at[pl.ds(t * PIECES, PIECES)], local_sem.at[0])
    own_x.start()

    def load_w(share, slot):
        return pltpu.make_async_copy(
            base_ref.at[pl.ds(pl.multiple_of(share * depth, depth), depth)],
            wbuf.at[slot],
            w_sem.at[slot],
        )

    def share(dz, other):
        return (z + dz) * 2 + (1 - x if other else x)

    own_down = pltpu.make_async_copy(down_mine, down.at[:, pl.ds(0, rank)], local_sem.at[1])
    own_up = pltpu.make_async_copy(up_mine, up.at[:, pl.ds(0, rank)], local_sem.at[2])
    pair_down = pltpu.make_async_remote_copy(
        src_ref=down_send, dst_ref=down.at[:, pl.ds(rank, rank)],
        send_sem=pair_send.at[0], recv_sem=pair_recv.at[0],
        device_id={"store": 1 - core}, device_id_type=MESH,
    )
    pair_up = pltpu.make_async_remote_copy(
        src_ref=up_send, dst_ref=up.at[:, pl.ds(rank, rank)],
        send_sem=pair_send.at[1], recv_sem=pair_recv.at[1],
        device_id={"store": 1 - core}, device_id_type=MESH,
    )

    def piece(which, p, way, target):
        i = which * PIECES + p
        return pltpu.make_async_remote_copy(
            src_ref=xbuf.at[i], dst_ref=xbuf.at[i],
            send_sem=send_sem.at[way], recv_sem=recv_sem.at[i],
            device_id={"tensor": target}, device_id_type=MESH,
        )

    def to_far(which, p):
        piece(which, p, 0, far).start()

    def to_near(which, p):
        piece(which, p, 1, near).start()

    def to_across(which, p):
        piece(which, p, 2, across).start()

    def got(which, p):
        piece(which, p, 2, across).wait_recv()

    def drain(way, count):
        view = xbuf.at[pl.ds(0, count)]
        pltpu.make_async_remote_copy(
            src_ref=view, dst_ref=view, send_sem=send_sem.at[way], recv_sem=recv_sem.at[0],
            device_id={"tensor": across}, device_id_type=MESH,
        ).wait_send()

    def product(which, first, count, slot, tile):
        lhs = xbuf[pl.ds(which * PIECES + first, count)].reshape(count * xbuf.shape[1], depth)
        columns = pl.ds(pl.multiple_of(tile * TILE, TILE), TILE)
        return jnp.dot(lhs, wbuf[slot, :, columns], preferred_element_type=F32)

    def add(which, first, count, slot, tile):
        rows = pl.ds(pl.multiple_of(first * xbuf.shape[1], xbuf.shape[1]), count * xbuf.shape[1])
        columns = pl.ds(pl.multiple_of(tile * TILE, TILE), TILE)
        total[rows, columns] += product(which, first, count, slot, tile)

    def set_own(tile):
        columns = pl.ds(pl.multiple_of(tile * TILE, TILE), TILE)
        total[:, columns] = product(t, 0, PIECES, 0, tile)

    def own_tiles(p):
        @pl.when(p == 0)
        def _():
            load_w(t, 0).wait()

        @pl.when(p < tiles // 2)
        def _():
            set_own(2 * p)
            set_own(2 * p + 1)

    def run(low, high, order):
        def one(u, carry):
            which, slot = order[0]
            for k in range(1, len(order)):
                which = jnp.where(u >= k * tiles, order[k][0], which)
                slot = jnp.where(u >= k * tiles, order[k][1], slot)

            @pl.when(u % tiles == 0)
            def _():
                load_w(which, slot).wait()

            add(which, 0, PIECES, slot, u % tiles)
            return carry

        top = len(order) * tiles
        lax.fori_loop(jnp.minimum(low, top), jnp.minimum(high, top), one, 0)

    def out_copy(h):
        rows = pl.ds(pl.multiple_of(h * 256, 256), 256)
        return pltpu.make_async_copy(wbuf.at[2, rows], out_ref.at[rows], out_sem.at[h])

    def finish(which, slot, h):
        def one(tile, carry):
            rows = pl.ds(pl.multiple_of(h * 256, 256), 256)
            columns = pl.ds(pl.multiple_of(tile * TILE, TILE), TILE)
            value = total[rows, columns] + product(which, 2 * h, 2, slot, tile)
            wbuf[2, rows, columns] = value.astype(BF16)
            return carry

        lax.fori_loop(0, tiles, one, 0)
        out_copy(h).start()

    def rank_partial():
        own_down.wait()
        pair_down.wait_recv()

        def one(b, carry):
            both = lax.dot_general(
                down[b], xbuf[t * PIECES + b], (((1,), (1,)), ((), ())), preferred_element_type=F32
            )
            part[b] = both[:rank] + both[rank:]
            return carry

        lax.fori_loop(0, n, one, 0)

        def send(d, carry):
            rs_copy(d).start()
            return carry

        lax.fori_loop(1, n, send, 0)

    def rs_copy(d):
        target = lax.rem(t + d, n)
        return pltpu.make_async_remote_copy(
            src_ref=part.at[target], dst_ref=gathered.at[t],
            send_sem=rs_send.at[d], recv_sem=rs_recv.at[d],
            device_id={"tensor": target}, device_id_type=MESH,
        )

    def ag_copy(d):
        target = lax.rem(t + d, n)
        return pltpu.make_async_remote_copy(
            src_ref=ranks.at[t], dst_ref=ranks.at[t],
            send_sem=ag_send.at[d], recv_sem=ag_recv.at[d],
            device_id={"tensor": target}, device_id_type=MESH,
        )

    def rank_sum():
        def got_part(d, value):
            rs_copy(d).wait_recv()
            return value + gathered[lax.rem(t - d + n, n)]

        value = lax.fori_loop(1, n, got_part, part[t])
        ranks[t] = value.astype(BF16)

        def send(d, carry):
            ag_copy(d).start()
            return carry

        lax.fori_loop(1, n, send, 0)

    def expand():
        own_up.wait()
        pair_up.wait_recv()

        def got_rank(d, carry):
            ag_copy(d).wait_recv()
            return carry

        lax.fori_loop(1, n, got_rank, 0)

        def one(b, carry):
            low = ranks[b].astype(F32).T.astype(BF16)
            both = jnp.concatenate([low, low], axis=1)
            rows = pl.ds(pl.multiple_of(b * 128, 128), 128)

            def tile(k, inner):
                columns = pl.ds(pl.multiple_of(k * TILE, TILE), TILE)
                total[rows, columns] += jnp.dot(
                    both, up[b, :, columns], preferred_element_type=F32
                )
                return inner

            lax.fori_loop(0, tiles, tile, 0)
            return carry

        lax.fori_loop(0, n, one, 0)

    def loop(count, body):
        def step(p, carry):
            body(p)
            return carry

        lax.fori_loop(0, count, step, 0)

    load_w(t, 0).start()
    own_down.start()
    own_up.start()
    pl.semaphore_wait(barrier, n)
    own_x.wait()

    @pl.when(is_end)
    def _():
        def first(p):
            to_far(t, p)
            to_across(t, p)

        loop(PIECES, first)

    @pl.when(jnp.logical_not(is_end))
    def _():
        def first(p):
            to_near(t, p)
            to_far(t, p)
            to_across(t, p)

        loop(PIECES, first)

    pair_down.start()
    pair_up.start()

    @pl.when(is_end)
    def _():
        f1, f2, f3 = share(sign, False), share(2 * sign, False), share(3 * sign, False)
        x0, x1 = share(0, True), share(sign, True)
        x2, x3 = share(2 * sign, True), share(3 * sign, True)
        load_w(f1, 1).start()
        load_w(x0, 2).start()

        def phase0(p):
            got(f1, p)
            to_across(f1, p)
            got(x0, p)

            @pl.when(p % 2 == 1)
            def _():
                to_far(x0, p)

            own_tiles(p)

        loop(PIECES, phase0)
        load_w(f2, 0).start()
        rank_partial()

        def phase1(p):
            got(f2, p)
            to_across(f2, p)
            got(x1, p)
            run(4 * p, 4 * p + 4, [(f1, 1), (x0, 2)])

        loop(PIECES, phase1)
        load_w(x1, 1).start()
        load_w(f3, 2).start()
        rank_sum()

        def phase2(p):
            got(f3, p)

            @pl.when(p % 2 == 0)
            def _():
                to_across(f3, p)

            got(x2, p)
            run(4 * p, 4 * p + 4, [(f2, 0), (x1, 1)])

            @pl.when(p == 4)
            def _():
                load_w(x2, 0).start()

            @pl.when(p == 1)
            def _():
                load_w(f3, 2).wait()

            @pl.when(p % 2 == 1)
            def _():
                loop(tiles, lambda k: add(f3, p - 1, 2, 2, k))

        loop(PIECES, phase2)
        load_w(x3, 1).start()
        expand()
        run(0, tiles, [(x2, 0)])
        load_w(x3, 1).wait()

        def phase3(h):
            got(x3, 2 * h)
            got(x3, 2 * h + 1)
            finish(x3, 1, h)

        loop(PIECES // 2, phase3)
        drain(0, 12)
        drain(2, 28)

    @pl.when(jnp.logical_not(is_end))
    def _():
        f1, f2, n1 = share(sign, False), share(2 * sign, False), share(-sign, False)
        x0, x1 = share(0, True), share(sign, True)
        xn, x2 = share(-sign, True), share(2 * sign, True)
        load_w(f1, 1).start()
        load_w(n1, 2).start()

        def phase0(p):
            got(f1, p)
            to_near(f1, p)
            to_across(f1, p)
            got(n1, p)
            to_far(n1, p)

            @pl.when(p % 2 == 0)
            def _():
                to_across(n1, p)

            got(x0, p)
            own_tiles(p)

        loop(PIECES, phase0)
        load_w(x0, 0).start()
        rank_partial()

        def phase1(p):
            got(f2, p)
            to_near(f2, p)

            @pl.when(p % 2 == 0)
            def _():
                to_across(f2, p)

            got(xn, p)

            @pl.when(p % 2 == 1)
            def _():
                to_far(xn, p)

            got(x1, p)
            run(6 * p, 6 * p + 6, [(f1, 1), (n1, 2), (x0, 0)])

            @pl.when(p == 3)
            def _():
                load_w(f2, 1).start()

            @pl.when(p == 5)
            def _():
                load_w(x1, 2).start()

        loop(PIECES, phase1)
        load_w(xn, 0).start()
        rank_sum()

        def phase2(h):
            got(x2, 2 * h)
            got(x2, 2 * h + 1)
            to_near(x2, 2 * h + 1)
            run(12 * h, 12 * h + 12, [(f2, 1), (x1, 2), (xn, 0)])

            @pl.when(h == 2)
            def _():
                load_w(x2, 1).start()

        loop(PIECES // 2, phase2)
        expand()
        load_w(x2, 1).wait()
        loop(PIECES // 2, lambda h: finish(x2, 1, h))
        drain(0, 20)
        drain(1, 28)
        drain(2, 24)

    pair_down.wait_send()
    pair_up.wait_send()

    def sent(d, carry):
        rs_copy(d).wait_send()
        ag_copy(d).wait_send()
        return carry

    lax.fori_loop(1, n, sent, 0)
    loop(PIECES // 2, lambda h: out_copy(h).wait())


def factors(adapter_shrink_weight, adapter_expand_weight, block_adapter_index):
    stores = lax.axis_size("store")
    me = lax.axis_index("store")
    held = adapter_shrink_weight.shape[0]
    step_count = block_adapter_index.shape[0]
    wanted = block_adapter_index.reshape(step_count, stores, -1).transpose(1, 0, 2)
    wanted = wanted.reshape(stores, -1)

    def pick(weight, index):
        kept = (index // held == me)[:, None, None]
        return jnp.where(kept, jnp.take(weight, index % held, axis=0), jnp.zeros((), BF16))

    mine = lax.dynamic_index_in_dim(wanted, me, 0, keepdims=False)
    other = lax.dynamic_index_in_dim(wanted, 1 - me, 0, keepdims=False)
    return tuple(
        pick(weight, index)
        for weight in (adapter_shrink_weight, adapter_expand_weight)
        for index in (mine, other)
    )


def fused(inputs, base_up_matrix, adapter_shrink_weight, adapter_expand_weight, block_adapter_index):
    step_count, rows_dev, depth = inputs.shape
    n = lax.axis_size("tensor")
    rows, hidden = step_count * rows_dev, base_up_matrix.shape[1]
    rank = adapter_shrink_weight.shape[1]
    block = rows // PIECES
    parts = factors(adapter_shrink_weight, adapter_expand_weight, block_adapter_index)
    out = pl.pallas_call(
        kernel,
        out_shape=jax.ShapeDtypeStruct((rows, hidden), BF16),
        in_specs=[pl.BlockSpec(memory_space=pl.ANY)] * 6,
        out_specs=pl.BlockSpec(memory_space=pl.ANY),
        scratch_shapes=[
            pltpu.VMEM((n * PIECES, block, depth), BF16),
            pltpu.VMEM((rows, hidden), F32),
            pltpu.VMEM((3, depth, hidden), BF16),
            pltpu.VMEM((PIECES, 2 * rank, depth), BF16),
            pltpu.VMEM((PIECES, 2 * rank, hidden), BF16),
            pltpu.VMEM((PIECES, rank, block), F32),
            pltpu.VMEM((PIECES, rank, block), F32),
            pltpu.VMEM((PIECES, rank, block), BF16),
            pltpu.SemaphoreType.DMA((3,)),
            pltpu.SemaphoreType.DMA((n * PIECES,)),
            pltpu.SemaphoreType.DMA((3,)),
            pltpu.SemaphoreType.DMA((3,)),
            pltpu.SemaphoreType.DMA((2,)),
            pltpu.SemaphoreType.DMA((2,)),
            pltpu.SemaphoreType.DMA((n,)),
            pltpu.SemaphoreType.DMA((n,)),
            pltpu.SemaphoreType.DMA((n,)),
            pltpu.SemaphoreType.DMA((n,)),
            pltpu.SemaphoreType.DMA((4,)),
        ],
        compiler_params=pltpu.CompilerParams(
            collective_id=0, has_side_effects=True, vmem_limit_bytes=63 * 1024 * 1024
        ),
        cost_estimate=pl.CostEstimate(
            flops=2 * rows * hidden * depth * n, bytes_accessed=100_000_000, transcendentals=0
        ),
    )(inputs.reshape(PIECES, block, depth), base_up_matrix, *parts)
    return out.reshape(step_count, rows_dev, hidden)


def general(
    inputs, base_up_matrix, adapter_shrink_weight, adapter_expand_weight, block_adapter_index
):
    step_count, rows_dev, width_dev = inputs.shape
    hidden_dev = base_up_matrix.shape[1]
    blocks_dev = block_adapter_index.shape[1] // lax.axis_size("store")
    block_rows = rows_dev // blocks_dev
    parts = factors(adapter_shrink_weight, adapter_expand_weight, block_adapter_index)
    swap = [(0, 1), (1, 0)]
    down = parts[0] + lax.ppermute(parts[1], "store", swap)
    up = parts[2] + lax.ppermute(parts[3], "store", swap)
    full_rows = lax.all_gather(
        inputs.reshape(step_count * rows_dev, width_dev), "tensor", axis=1, tiled=True
    )
    own_blocks = inputs.reshape(step_count * blocks_dev, block_rows, width_dev)
    low_rank = jnp.einsum("btd,brd->brt", own_blocks, down, preferred_element_type=F32)
    low_rank = lax.psum(low_rank, "tensor").astype(BF16)
    base_out = jnp.dot(full_rows, base_up_matrix, preferred_element_type=F32)
    adapter_out = jnp.einsum("brt,brf->btf", low_rank, up, preferred_element_type=F32)
    projected = (base_out + adapter_out.reshape(base_out.shape)).astype(BF16)
    return projected.reshape(step_count, rows_dev, hidden_dev)


def solution(mesh):
    placed = (
        P("groups", "store", "tensor"),
        P(None, "tensor"),
        P("store", None, "tensor"),
        P("store", None, "tensor"),
        P("groups", None),
    )
    small = mesh.shape["tensor"] == PIECES and mesh.shape["store"] == 2
    return jax.shard_map(
        fused if small else general,
        mesh=mesh, in_specs=placed, out_specs=P("groups", "store", "tensor"), check_vma=False,
    )
```

time: 468 us -> 241 us (0.51)
  waiting for transfers between devices: 324 us -> 0 us
  Pallas kernels: 0 us -> 201 us
  matrix products: 87.6 us -> 0 us
  blocking collectives: 16.3 us -> 0 us
  local copies, waits for them, and re-layouts: 13 us -> 28.6 us
  between operations: 13.4 us -> 0.06 us
    all_gather x2 -> x0, waiting for transfers between devices: 323 us -> none  [the longest x1 228 us: local(): lax.all_gather(flat_rows, 'tensor', axis=1, tiled=True)]
    pallas_call x0 -> x1, Pallas kernels: none -> 201 us  [fused(): pl.pallas_call(kernel, out_shape=jax.ShapeDtypeStruct((rows, hidden), BF1...]
    dot_general x2 -> x0, matrix products: 87.6 us -> none  [the longest x1 71.5 us: local(): jnp.dot(full_rows, base_up_matrix, preferred_element_type=jnp.float32)]
    all_to_all x2 -> x0, blocking collectives: 16.3 us -> none  [the longest x1 10.9 us: local(): lax.all_to_all(expand_transfer, 'store', split_axis=0, concat_axis=0, til...]
    gather x2 -> x4, local copies, waits for them, and re-layouts: 12.1 us -> 21.2 us  [pick(): jnp.take(weight, index % held, axis=0)]
    reduce_sum x2 -> x0, other arithmetic: 9.06 us -> none  [the longest x1 7.33 us: local(): jnp.sum(got_up.astype(jnp.float32), axis=0).astype(jnp.bfloat16)]
    unnamed x0 -> x1, local copies, waits for them, and re-layouts: none -> 6.6 us
    select_n x2 -> x4, other arithmetic: 5 us -> 11.1 us  [pick(): jnp.where(kept, jnp.take(weight, index % held, axis=0), jnp.zeros((), BF16))]
  transfers between devices with their start and end apart: 2 -> 0, of which waited for: 2 -> 0; matrix products, arithmetic and copies ran while one was open for 5% -> 0% of each run, Pallas kernels for 0% -> 0%
where the time goes in v1:
time: 241 us
  Pallas kernels  201 us (83%)
  local copies, waits for them, and re-layouts  28.6 us (12%)
  other arithmetic  11.1 us (5%)
    pallas_call x1, Pallas kernels, fused(): pl.pallas_call(kernel, out_shape=jax.ShapeDtypeStruct((rows, hidden), BF1...  201 us
    gather x4, local copies, waits for them, and re-layouts, pick(): jnp.take(weight, index % held, axis=0)  21.2 us
    select_n x4, other arithmetic, pick(): jnp.where(kept, jnp.take(weight, index % held, axis=0), jnp.zeros((), BF16))  11.1 us
    unnamed x1, local copies, waits for them, and re-layouts  6.6 us

profile of v1, /device:TPU:0, one launch (start us, length us, event | category | flops | bytes accessed | tf_op | source)
XLA Modules:
  0.0 240.7 jit_solution(17329448792701104071)
XLA Ops:
  0.0 0.8 reshape.81
  0.8 0.1 reshape.82
  0.9 2.8 %gather_fusion = bf16[8,64,1024]{2,1,0:T(8,128)(2,1)S(1)} fusion(bf16[32,64,1024]{2,1,0:T(8,128)(2,1)} %param.11, s32[1024]{0:T(1024)S(1)} %pad_clamp_fusion.1), kind=kCustom, calls=%fused_computation.clone | custom fusion | bytes 2097184 | tf_op jit(solution)/shard_map/jit(_take)/gather | solution.py:426
  3.7 1.2 select_select_fusion.3.down_mine
  4.9 2.8 %gather_fusion.1 = bf16[8,64,1024]{2,1,0:T(8,128)(2,1)S(1)} fusion(bf16[32,64,1024]{2,1,0:T(8,128)(2,1)} %param.11, s32[1024]{0:T(1024)S(1)} %pad_clamp_fusion), kind=kCustom, calls=%fused_computation.2.clone | custom fusion | bytes 2097184 | tf_op jit(solution)/shard_map/jit(_take)/gather | solution.py:426
  7.7 1.2 select_select_fusion.2.down_send
  8.9 7.8 %gather_fusion.3 = bf16[8,64,3584]{2,1,0:T(8,128)(2,1)} fusion(bf16[32,64,3584]{2,1,0:T(8,128)(2,1)} %param.12, s32[1024]{0:T(1024)S(1)} %pad_clamp_fusion), kind=kCustom, calls=%fused_computation.3.clone | custom fusion | bytes 7340064 | tf_op jit(solution)/shard_map/jit(_take)/gather | solution.py:426
  16.7 4.4 %select_select_fusion.up_send = bf16[8,64,3584]{2,1,0:T(8,128)(2,1)} fusion(bf16[8,64,3584]{2,1,0:T(8,128)(2,1)} %gather_fusion.3, pred[8]{0:T(512)(128)(4,1)S(1)} %get-tuple-element.9, pred[8]{0:T(512)(128)(4,1)S(1)} %get-tuple-element.6), kind=kLoop, calls=%fused_computation.4 | loop fusion | flops 3670016 | bytes 7340048 | tf_op jit(solution)/shard_map/jit(_where)/select_n | solution.py:426
  21.1 7.8 %gather_fusion.2 = bf16[8,64,3584]{2,1,0:T(8,128)(2,1)} fusion(bf16[32,64,3584]{2,1,0:T(8,128)(2,1)} %param.12, s32[1024]{0:T(1024)S(1)} %pad_clamp_fusion.1), kind=kCustom, calls=%fused_computation.1.clone | custom fusion | bytes 7340064 | tf_op jit(solution)/shard_map/jit(_take)/gather | solution.py:426
  28.9 4.3 %select_select_fusion.1.up_mine = bf16[8,64,3584]{2,1,0:T(8,128)(2,1)} fusion(bf16[8,64,3584]{2,1,0:T(8,128)(2,1)} %gather_fusion.2, pred[8]{0:T(512)(128)(4,1)S(1)} %get-tuple-element.17, pred[8]{0:T(512)(128)(4,1)S(1)} %get-tuple-element.15), kind=kLoop, calls=%fused_computation.5 | loop fusion | flops 3670016 | bytes 7340048 | tf_op jit(solution)/shard_map/jit(_where)/select_n | solution.py:426
  33.2 200.9 %shard_map.55 = bf16[1024,3584]{1,0:T(8,128)(2,1)} custom-call(bf16[8,128,1024]{2,1,0:T(8,128)(2,1)} %bitcast.33, bf16[8192,3584]{1,0:T(8,128)(2,1)} %base_ref.1, bf16[8,64,1024]{2,1,0:T(8,128)(2,1)} %select_select_fusion.3.down_mine, bf16[8,64,1024]{2,1,0:T(8,128)(2,1)} %select_select_fusion.2.down_send, bf16[8,64,3584]{2,1,0:T(8,128)(2,1)} %select_select_fusion.1.up_mine, ...), custom_call_target="tpu_custom_call" | custom-call | flops 60129542144 | bytes 100000000 | tf_op jit(solution)/shard_map/pallas_call | solution.py:444
  234.1 6.6 %copy.8 = bf16[2,512,3584]{2,1,0:T(8,128)(2,1)} copy(bf16[2,512,3584]{2,1,0:T(8,128)(2,1)} %bitcast.31) | data formatting | bytes 14680064
  (5 shorter events, 0.0 us)
